TPU v7x, 32 devices: a whole 2x2x4 slice. The times are simulated.
32 devices in a mesh: grid: 2 (over y), row: 4 (over x, core), col: 4 (over z).
Axes of the slice: x: 2, y: 2, z: 4, core: 2. Of those that a mesh axis runs over, the one named last changes fastest.
Arguments:
- schur: bfloat16 [2, 4096, 4096], P('grid', 'row', 'col'), may hold values from -6 to 6
- d_inv: bfloat16 [1, 2, 1024, 1024], P(None, 'grid', None, 'col'), may hold values from -0.0009765625 to 0.0087890625, as said below
- blocks: int32 [1, 2, 12], P(None, 'grid'), may hold values from 0 to 15, as said below
Outputs:
- merged: bfloat16 [2, 2048, 4096], P('grid', 'row', 'col')
Inputs may be any that keep to these rules, and one draw needn't show every extreme that they name: blocks[l, g] is the same for all grids g of one group of 2^l grids at level l. Entry k < 4 lies in k * 4 to (k + 1) * 4 - 1; the other 8 entries are distinct blocks, none of them a pivot block of that list. d_inv[l, g] is the same for all grids g of one group of 2^l grids at level l.
All inputs are finite; a program needn't handle non-finite values.
Results may differ from a plain program's by a relative error of at most 0.0067.
Values may be sent and summed in bfloat16 or wider, within the bound.
A program may use at most 64 MiB of HBM per device.

v0:
```python
import jax
import jax.numpy as jnp
from jax import lax
from jax.sharding import PartitionSpec as P


def swapped(block, axis, apart):
    count = lax.axis_size(axis)
    route = []
    for low in range(count):
        high = low | 1 << apart
        if high != low and high < count:
            route += [(low, high), (high, low)]
    return lax.ppermute(block, axis, route)


def unchanged(tile_rows, other_rows):
    return tile_rows


def shards(schur, d_inv, blocks):
    n_rows = lax.axis_size("row")
    grid_pos = lax.axis_index("grid")
    row_pos = lax.axis_index("row")
    col_pos = lax.axis_index("col")
    levels = blocks.shape[0]
    current = schur[0].astype(jnp.float32)
    quarter_rows = current.shape[0]
    local_cols = current.shape[1]
    width = d_inv.shape[2]
    block = width // n_rows
    col_start = col_pos * local_cols
    col_ids = (col_start + jnp.arange(local_cols, dtype=jnp.int32)) // block
    row_shift = jnp.zeros((), jnp.int32)
    for height in range(levels):
        rows_here = current.shape[0]
        count = rows_here // block
        chosen = blocks[height, 0]
        pivots = chosen[:n_rows]
        listed = chosen[n_rows:]
        row_start = row_pos * quarter_rows + row_shift
        col_keep = jnp.any(col_ids[:, None] == listed[None, :], axis=1)
        row_ids = row_start // block + jnp.arange(count, dtype=jnp.int32)
        row_keep = jnp.any(row_ids[:, None] == listed[None, :], axis=1)
        left_piece = lax.dynamic_slice_in_dim(
            current, pivots[col_pos] * block - col_start, block, 1
        ).astype(jnp.bfloat16)
        left_panel = lax.all_gather(left_piece, "col", axis=1, tiled=True)
        offset = pivots[row_pos] * block - row_start
        owned = (offset >= 0) & (offset < rows_here)
        upper_piece = lax.dynamic_slice_in_dim(
            current, jnp.clip(offset, 0, rows_here - block), block, 0
        )
        upper_piece = jnp.where(owned, upper_piece, 0.0).astype(jnp.bfloat16)
        for member_bit in range(height):
            upper_piece = upper_piece + swapped(upper_piece, "grid", member_bit)
        upper_panel = lax.all_gather(upper_piece, "row", axis=0, tiled=True)
        upper_panel = jnp.where(col_keep[None, :], upper_panel, jnp.zeros((), jnp.bfloat16))
        inverse_part = d_inv[height, 0]
        pieces = []
        inverse_full = lax.all_gather(inverse_part, "col", axis=1, tiled=True)

        def update_block(tile_rows, left_rows):
            scaled = jnp.dot(left_rows, inverse_full, preferred_element_type=jnp.float32).astype(
                jnp.bfloat16
            )
            return tile_rows - jnp.dot(scaled, upper_panel, preferred_element_type=jnp.float32)

        for position in range(count):
            tile_rows = current[position * block : (position + 1) * block]
            left_rows = left_panel[position * block : (position + 1) * block]
            pieces.append(
                lax.cond(row_keep[position], update_block, unchanged, tile_rows, left_rows)
            )
        updated = jnp.concatenate(pieces, axis=0).astype(jnp.bfloat16)
        bit_value = grid_pos >> height & 1
        half_rows = rows_here // 2
        kept = lax.dynamic_slice_in_dim(updated, bit_value * half_rows, half_rows, 0)
        given = lax.dynamic_slice_in_dim(updated, (1 - bit_value) * half_rows, half_rows, 0)
        received = swapped(given, "grid", height)
        current = kept.astype(jnp.float32) + received.astype(jnp.float32)
        row_shift = row_shift + bit_value * half_rows
    return current.astype(jnp.bfloat16)[None]


def solution(mesh):
    return jax.shard_map(
        shards,
        mesh=mesh,
        in_specs=(P("grid", "row", "col"), P(None, "grid", None, "col"), P(None, "grid", None)),
        out_specs=P("grid", "row", "col"),
        check_vma=False,
    )
```

profile of v0, /device:TPU:0, one launch (start us, length us, event | category | flops | bytes accessed | tf_op | source)
XLA Modules:
  0.0 185.3 jit_solution(8657682813546505551)
XLA Ops:
  6.5 1.4 constant_dynamic-slice_fusion.1
  8.6 4.0 %convert_element_type.64 = f32[1,1024,1024]{2,1,0:T(8,128)} convert(bf16[1,1024,1024]{2,1,0:T(8,128)(2,1)} %param.11) | non-fusion elementwise | flops 1048576 | bytes 6291456 | tf_op jit(solution)/shard_map/convert_element_type | solution.py:27
  12.6 2.2 %select_convert_fusion = bf16[1,256,1024]{2,1,0:T(8,128)(2,1)} fusion(f32[1,1024,1024]{2,1,0:T(8,128)} %convert_element_type.64, s32[]{:T(128)S(6)} %min.4, pred[]{:T(512)S(6)} %and.29), kind=kLoop, calls=%fused_computation.20 | loop fusion | flops 262144 | bytes 1048581 | tf_op jit(solution)/shard_map/convert_element_type | solution.py:54
  15.5 2.1 %dynamic-slice_convert_fusion = bf16[1,1024,256]{2,1,0:T(8,128)(2,1)} fusion(f32[1,1024,1024]{2,1,0:T(8,128)} %convert_element_type.64, s32[]{:T(128)S(6)} %select_n.45), kind=kLoop, calls=%fused_computation.21 | loop fusion | bytes 1048580 | tf_op jit(solution)/shard_map/convert_element_type | solution.py:47
  17.6 0.7 all-gather.9.cloned.1.call-update
  18.3 0.1 slice_bitcast_fusion.4
  18.4 0.2 compare_reduce_fusion.1
  18.6 0.6 fusion.12
  21.6 0.1 compare_reduce_fusion
  21.7 3.7 %slice_bitcast_fusion.3 = (f32[256,1024]{1,0:T(8,128)}, f32[256,1024]{1,0:T(8,128)S(1)}, f32[256,1024]{1,0:T(8,128)S(1)}, f32[256,1024]{1,0:T(8,128)S(1)}) fusion(f32[1,1024,1024]{2,1,0:T(8,128)} %convert_element_type.64), kind=kLoop, calls=%fused_computation.19 | loop fusion | bytes 8388608 | tf_op jit(solution)/shard_map/slice | solution.py:70
  25.4 14.8 %all-gather.11.cloned.1.call-done = bf16[1,1024,1024]{2,1,0:T(8,128)(2,1)} async-done(((bf16[1,256,1024]{2,1,0:T(8,128)(2,1)}), bf16[1,1024,1024]{2,1,0:T(8,128)(2,1)}) %all-gather.11.cloned.1.call-update) | async-done | bytes 2097168 | tf_op jit(solution)/shard_map/all_gather | solution.py:57
  40.2 3.1 %bitcast_select_fusion = bf16[1024,1024]{1,0:T(8,128)(2,1)} fusion(bf16[1,1024,1024]{2,1,0:T(8,128)(2,1)} %all-gather.11.cloned.1.call-done, pred[1024]{0:T(1024)(128)(4,1)S(1)} %compare_reduce_fusion), kind=kLoop, calls=%fused_computation.13 | loop fusion | flops 1048576 | bytes 4195328 | tf_op jit(solution)/shard_map/jit(_where)/select_n | solution.py:58
  43.3 44.8 %all-gather.7.cloned.1.call-done = bf16[1,1024,1024]{2,1,0:T(8,128)(2,1)} async-done(((bf16[1,1024,256]{2,1,0:T(8,128)(2,1)}), bf16[1,1024,1024]{2,1,0:T(8,128)(2,1)}) %all-gather.7.cloned.1.call-update) | async-done | bytes 2097168 | tf_op jit(solution)/shard_map/all_gather | solution.py:48
  88.1 46.1 %all-gather.9.cloned.1.call-done = bf16[1,1,1024,1024]{3,2,1,0:T(8,128)(2,1)} async-done(((bf16[1,1,1024,256]{3,2,1,0:T(8,128)(2,1)}), bf16[1,1,1024,1024]{3,2,1,0:T(8,128)(2,1)}) %all-gather.9.cloned.1.call-update) | async-done | bytes 2097168 | tf_op jit(solution)/shard_map/all_gather | solution.py:61
  134.1 2.1 %convert.16 = bf16[256,1024]{1,0:T(8,128)(2,1)} convert(f32[256,1024]{1,0:T(8,128)} %get-tuple-element.83) | non-fusion elementwise | flops 262144 | bytes 1572864 | tf_op jit(solution)/shard_map/convert.4
  136.2 0.9 convert.17
  137.1 0.9 convert.18
  138.1 1.0 copy-done
  139.0 0.2 copy-done.1
  139.2 1.2 pad_maximum_fusion
  140.4 0.1 constant_dynamic-slice_fusion
  140.5 11.8 %collective-permute-start = (bf16[512,1024]{1,0:T(8,128)(2,1)S(1)}, bf16[512,1024]{1,0:T(8,128)(2,1)}, u32[]{:S(2)}, u32[]{:S(2)}) collective-permute-start(bf16[512,1024]{1,0:T(8,128)(2,1)S(1)} %constant_dynamic-slice_fusion), channel_id=1, source_target_pairs={{0,16},{16,0},{1,17},{17,1},{2,18},{18,2},{3,19},{19,3},{4,20},{20... | collective-permute-start | bytes 3145736 | tf_op jit(solution)/shard_map/ppermute | solution.py:14
  152.3 24.0 %collective-permute-done = bf16[512,1024]{1,0:T(8,128)(2,1)} collective-permute-done((bf16[512,1024]{1,0:T(8,128)(2,1)S(1)}, bf16[512,1024]{1,0:T(8,128)(2,1)}, u32[]{:S(2)}, u32[]{:S(2)}) %collective-permute-start) | collective-permute-done | bytes 1048608 | tf_op jit(solution)/shard_map/ppermute | solution.py:14
  176.2 2.6 %fusion.8 = bf16[1,512,1024]{2,1,0:T(8,128)(2,1)} fusion(bf16[512,1024]{1,0:T(8,128)(2,1)} %collective-permute-done, bf16[1024,1024]{1,0:T(8,128)(2,1)S(1)} %pad_maximum_fusion, s32[]{:T(128)S(6)} %select_n.51), kind=kLoop, calls=%fused_computation.15 | loop fusion | flops 2097152 | bytes 3145732 | tf_op jit(solution)/shard_map/broadcast_in_dim | solution.py:83
  (16 shorter events, 0.2 us)
Async XLA Ops:
  6.5 33.7 %all-gather.11.cloned.1.call-start = ((), (), s32[]{:S(2)}) async-start(), calls=%async_computation.2 | async-start | bytes 2621440 | tf_op jit(solution)/shard_map/all_gather | solution.py:57
  12.6 5.7 %copy-start.2 = (s32[1,1,12]{2,1,0:T(1,128)S(1)}, s32[1,1,12]{2,1,0:T(1,128)}, u32[]{:S(2)}) copy-start(s32[1,1,12]{2,1,0:T(1,128)} %param.13) | copy-start | bytes 148
  14.8 73.3 %all-gather.7.cloned.1.call-start = ((), (), s32[]{:S(2)}) async-start(), calls=%async_computation | async-start | bytes 2621440 | tf_op jit(solution)/shard_map/all_gather | solution.py:48
  17.6 116.6 %all-gather.9.cloned.1.call-start = ((), (), s32[]{:S(2)}) async-start(), calls=%async_computation.1 | async-start | bytes 2621440 | tf_op jit(solution)/shard_map/all_gather | solution.py:61
  138.0 1.0 copy-start
  138.0 1.2 copy-start.1
  140.5 35.7 %collective-permute-start = (bf16[512,1024]{1,0:T(8,128)(2,1)S(1)}, bf16[512,1024]{1,0:T(8,128)(2,1)}, u32[]{:S(2)}, u32[]{:S(2)}) collective-permute-start(bf16[512,1024]{1,0:T(8,128)(2,1)S(1)} %constant_dynamic-slice_fusion), channel_id=1, source_target_pairs={{0,16},{16,0},{1,17},{17,1},{2,18},{18,2},{3,19},{19,3},{4,20},{20... | collective-permute-start | bytes 3145736 | tf_op jit(solution)/shard_map/ppermute | solution.py:14
Sparse Core Ops, SparseCore 0:
  14.9 25.2 all-gather.10
  41.8 46.2 all-gather.6
  89.6 44.4 all-gather.8
where the time goes:
time: 184 us; the launch traced here: 185 us
  waiting for transfers between devices  130 us (71%)
  other arithmetic  17.3 us (9%)
  between operations  16.9 us (9%)
  starting transfers between devices  11.8 us (6%)
  local copies, waits for them, and re-layouts  8.99 us (5%)
    all_gather x1, waiting for transfers between devices, shards(): inverse_full = lax.all_gather(inverse_part, 'col', axis=1, tiled=True)  46.1 us
    all_gather x1, waiting for transfers between devices, shards(): left_panel = lax.all_gather(left_piece, 'col', axis=1, tiled=True)  44.8 us
    ppermute x1, waiting for transfers between devices, swapped(): return lax.ppermute(block, axis, route)  24 us
    all_gather x1, waiting for transfers between devices, shards(): upper_panel = lax.all_gather(upper_piece, 'row', axis=0, tiled=True)  14.8 us
    ppermute x1, starting transfers between devices, swapped(): return lax.ppermute(block, axis, route)  11.8 us
    convert_element_type x1, other arithmetic, shards(): current = schur[0].astype(jnp.float32)  4.02 us
    another operation x4, other arithmetic  3.92 us
  transfers between devices with their start and end apart: 4, of which 4 were waited for; matrix products, arithmetic and copies ran while one was open for 5% of the time, Pallas kernels for 0%

commit v1 on v0

v1 whole, which is shorter than its diff:
```python
import functools

import jax
import jax.numpy as jnp
from jax import lax
from jax.experimental import pallas as pl
from jax.experimental.pallas import tpu as pltpu
from jax.sharding import PartitionSpec as P

MESH = pl.DeviceIdType.MESH


def swapped(block, axis, apart):
    count = lax.axis_size(axis)
    route = []
    for low in range(count):
        high = low | 1 << apart
        if high != low and high < count:
            route += [(low, high), (high, low)]
    return lax.ppermute(block, axis, route)


def unchanged(tile_rows, other_rows):
    return tile_rows


def flipped(index, bits):
    bit = 1
    while bit <= bits:
        if bits & bit:
            index = index + bit - 2 * bit * lax.rem(lax.div(index, bit), 2)
        bit *= 2
    return index


class Gather:
    def __init__(self, axis, own, place, sems):
        self.count = lax.axis_size(axis)
        me = lax.axis_index(axis)
        self.copies = {}
        for s in range(1, self.count):
            low = s & -s
            rest = s ^ low
            held = flipped(me, rest)
            self.copies[s] = pltpu.make_async_remote_copy(
                src_ref=own if rest == 0 else place(held),
                dst_ref=place(held),
                send_sem=sems[0].at[s - 1],
                recv_sem=sems[1].at[s - 1],
                device_id={axis: flipped(me, low)},
                device_id_type=MESH,
            )
        self.waited = set()

    def start(self):
        for s in reversed(range(1, self.count)):
            if s & (s - 1) == 0:
                self.copies[s].start()

    def arrive(self, s):
        if s not in self.waited:
            self.waited.add(s)
            self.copies[s].wait_recv()

    def forward(self):
        for rest in reversed(range(2, self.count)):
            lows = [low for low in range(1, rest) if low & (low - 1) == 0 and low < (rest & -rest)]
            if lows:
                self.arrive(rest)
                for low in lows:
                    self.copies[rest | low].start()

    def finish(self):
        for s in range(1, self.count):
            self.arrive(s)

    def sent(self):
        for s in range(1, self.count):
            self.copies[s].wait_send()


def eliminate_kernel(
    chunk,
    tile_ref,
    left_ref,
    upper_ref,
    inv_ref,
    out_ref,
    tile,
    left,
    upper,
    inv,
    product,
    given,
    received,
    local_sems,
    inv_col_sems,
    inv_row_sems,
    upper_sems,
    left_sems,
    swap_sems,
):
    row_pos = lax.axis_index("row")
    col_pos = lax.axis_index("col")
    grid_pos = lax.axis_index("grid")
    n_rows = lax.axis_size("row")
    n_cols = lax.axis_size("col")
    rows = tile.shape[0]
    half = rows // 2
    per_half = half // chunk
    width = inv.shape[0]
    piece = left_ref.shape[1]
    slab = width // n_rows
    bit_value = lax.rem(grid_pos, 2)
    partner = flipped(grid_pos, 1)

    locals_ = [
        pltpu.make_async_copy(
            inv_ref.at[pl.ds(row_pos * slab, slab), :],
            inv.at[pl.ds(row_pos * slab, slab), pl.ds(pl.multiple_of(col_pos * piece, piece), piece)],
            local_sems.at[0],
        ),
        pltpu.make_async_copy(upper_ref, upper.at[pl.ds(row_pos * slab, slab), :], local_sems.at[1]),
        pltpu.make_async_copy(
            left_ref, left.at[:, pl.ds(pl.multiple_of(col_pos * piece, piece), piece)], local_sems.at[2]
        ),
        pltpu.make_async_copy(tile_ref, tile, local_sems.at[3]),
    ]
    for copy in locals_:
        copy.start()

    barrier = pltpu.get_barrier_semaphore()
    peers = [{"grid": partner}]
    for axis, count in (("row", n_rows), ("col", n_cols)):
        bit = 1
        while bit < count:
            peers.append({axis: flipped(lax.axis_index(axis), bit)})
            bit *= 2
    for peer in peers:
        pl.semaphore_signal(barrier, inc=1, device_id=peer, device_id_type=MESH)
    pl.semaphore_wait(barrier, len(peers))

    def inv_place(held):
        return inv.at[
            pl.ds(row_pos * slab, slab), pl.ds(pl.multiple_of(held * piece, piece), piece)
        ]

    def slab_place(held):
        return inv.at[pl.ds(held * slab, slab), :]

    def upper_place(held):
        return upper.at[pl.ds(held * slab, slab), :]

    starts = [(1 - bit_value) * half + i * chunk for i in range(per_half)]
    starts += [bit_value * half + i * chunk for i in range(per_half)]

    def left_gather(i):
        def place(held):
            return left.at[
                pl.ds(starts[i], chunk), pl.ds(pl.multiple_of(held * piece, piece), piece)
            ]

        return Gather(
            "col",
            left_ref.at[pl.ds(starts[i], chunk), :],
            place,
            (left_sems.at[0, i], left_sems.at[1, i]),
        )

    inv_col = Gather(
        "col",
        inv_ref.at[pl.ds(row_pos * slab, slab), :],
        inv_place,
        (inv_col_sems.at[0], inv_col_sems.at[1]),
    )
    inv_row = Gather(
        "row", slab_place(row_pos), slab_place, (inv_row_sems.at[0], inv_row_sems.at[1])
    )
    upper_all = Gather(
        "row", upper_ref, upper_place, (upper_sems.at[0], upper_sems.at[1])
    )
    lefts = [left_gather(i) for i in range(2 * per_half)]

    inv_col.start()
    upper_all.start()
    lefts[0].start()
    inv_col.forward()
    lefts[1].start()
    inv_col.finish()
    locals_[0].wait()
    inv_row.start()
    upper_all.forward()
    lefts[0].forward()
    lefts[2].start()
    inv_row.forward()
    lefts[1].forward()
    lefts[3].start()
    upper_all.finish()
    inv_row.finish()
    locals_[1].wait()

    @pl.loop(0, width // chunk)
    def _(i):
        at = pl.ds(pl.multiple_of(i * chunk, chunk), chunk)
        product[at, :] = jnp.dot(
            inv[at, :], upper[...], preferred_element_type=jnp.float32
        ).astype(jnp.bfloat16)

    locals_[2].wait()
    locals_[3].wait()

    def eliminated(i):
        at = pl.ds(pl.multiple_of(starts[i], chunk), chunk)
        change = jnp.dot(left[at, :], product[...], preferred_element_type=jnp.float32)
        return (tile[at, :].astype(jnp.float32) - change).astype(jnp.bfloat16)

    swaps = []
    for i in range(2 * per_half):
        ahead = i + 2
        if ahead < 2 * per_half:
            lefts[ahead].forward()
        if ahead + 2 < 2 * per_half:
            lefts[ahead + 2].start()
        lefts[i].finish()
        if i < per_half:
            at = pl.ds(i * chunk, chunk)
            given[at, :] = eliminated(i)
            swap = pltpu.make_async_remote_copy(
                src_ref=given.at[at, :],
                dst_ref=received.at[at, :],
                send_sem=swap_sems.at[0, i],
                recv_sem=swap_sems.at[1, i],
                device_id={"grid": partner},
                device_id_type=MESH,
            )
            swap.start()
            swaps.append(swap)
        else:
            at = pl.ds((i - per_half) * chunk, chunk)
            kept = eliminated(i).astype(jnp.float32)
            swaps[i - per_half].wait_recv()
            out_ref[at, :] = (kept + received[at, :].astype(jnp.float32)).astype(out_ref.dtype)
    for gather in [inv_col, inv_row, upper_all] + lefts:
        gather.sent()
    for swap in swaps:
        swap.wait_send()


def first_level(tile, inverse, chosen, out_dtype):
    n_rows = lax.axis_size("row")
    n_cols = lax.axis_size("col")
    rows, cols = tile.shape
    width = inverse.shape[0]
    block = width // n_rows
    row_start = lax.axis_index("row") * rows
    col_pos = lax.axis_index("col")
    col_start = col_pos * cols
    pivots = chosen[:n_rows]
    listed = chosen[n_rows:]
    row_ids = (row_start + jnp.arange(rows, dtype=jnp.int32)) // block
    col_ids = (col_start + jnp.arange(cols, dtype=jnp.int32)) // block
    row_keep = jnp.any(row_ids[:, None] == listed[None, :], axis=1)
    col_keep = jnp.any(col_ids[:, None] == listed[None, :], axis=1)
    zero = jnp.zeros((), tile.dtype)
    left = lax.dynamic_slice_in_dim(tile, pivots[col_pos] * block - col_start, block, 1)
    left = jnp.where(row_keep[:, None], left, zero)
    upper = lax.dynamic_slice_in_dim(
        tile, pivots[lax.axis_index("row")] * block - row_start, block, 0
    )
    upper = jnp.where(col_keep[None, :], upper, zero)
    chunk = rows // 4
    bf16 = jnp.bfloat16
    dma = pltpu.SemaphoreType.DMA
    return pl.pallas_call(
        functools.partial(eliminate_kernel, chunk),
        out_shape=jax.ShapeDtypeStruct((rows // 2, cols), out_dtype),
        in_specs=[pl.BlockSpec(memory_space=pl.ANY)] * 4,
        out_specs=pl.BlockSpec(memory_space=pltpu.VMEM),
        scratch_shapes=[
            pltpu.VMEM((rows, cols), bf16),
            pltpu.VMEM((rows, width), bf16),
            pltpu.VMEM((width, cols), bf16),
            pltpu.VMEM((width, width), bf16),
            pltpu.VMEM((width, cols), bf16),
            pltpu.VMEM((rows // 2, cols), bf16),
            pltpu.VMEM((rows // 2, cols), bf16),
            dma((4,)),
            dma((2, n_cols - 1)),
            dma((2, n_rows - 1)),
            dma((2, n_rows - 1)),
            dma((2, 4, n_cols - 1)),
            dma((2, 2)),
        ],
        compiler_params=pltpu.CompilerParams(
            collective_id=0, has_side_effects=True, vmem_limit_bytes=40 * 1024 * 1024
        ),
    )(tile, left, upper, inverse)


def shards(schur, d_inv, blocks):
    n_rows = lax.axis_size("row")
    grid_pos = lax.axis_index("grid")
    row_pos = lax.axis_index("row")
    col_pos = lax.axis_index("col")
    levels = blocks.shape[0]
    quarter_rows = schur.shape[1]
    local_cols = schur.shape[2]
    width = d_inv.shape[2]
    block = width // n_rows
    col_start = col_pos * local_cols
    col_ids = (col_start + jnp.arange(local_cols, dtype=jnp.int32)) // block
    current = first_level(
        schur[0], d_inv[0, 0], blocks[0, 0], jnp.bfloat16 if levels == 1 else jnp.float32
    )
    row_shift = (grid_pos & 1) * (quarter_rows // 2)
    for height in range(1, levels):
        rows_here = current.shape[0]
        count = rows_here // block
        chosen = blocks[height, 0]
        pivots = chosen[:n_rows]
        listed = chosen[n_rows:]
        row_start = row_pos * quarter_rows + row_shift
        col_keep = jnp.any(col_ids[:, None] == listed[None, :], axis=1)
        left_piece = lax.dynamic_slice_in_dim(
            current, pivots[col_pos] * block - col_start, block, 1
        ).astype(jnp.bfloat16)
        left_panel = lax.all_gather(left_piece, "col", axis=1, tiled=True)
        part = min(block, rows_here)
        offset = pivots[row_pos] * block - row_start
        upper_piece = jnp.zeros((block, local_cols), jnp.bfloat16)
        for start in range(0, block, part):
            inside = offset + start
            owned = (inside >= 0) & (inside < rows_here)
            rows_of = lax.dynamic_slice_in_dim(
                current, jnp.clip(inside, 0, rows_here - part), part, 0
            )
            upper_piece = lax.dynamic_update_slice_in_dim(
                upper_piece, jnp.where(owned, rows_of, 0.0).astype(jnp.bfloat16), start, 0
            )
        for member_bit in range(height):
            upper_piece = upper_piece + swapped(upper_piece, "grid", member_bit)
        upper_panel = lax.all_gather(upper_piece, "row", axis=0, tiled=True)
        upper_panel = jnp.where(col_keep[None, :], upper_panel, jnp.zeros((), jnp.bfloat16))
        inverse_full = lax.all_gather(d_inv[height, 0], "col", axis=1, tiled=True)

        def update_block(tile_rows, left_rows):
            scaled = jnp.dot(left_rows, inverse_full, preferred_element_type=jnp.float32).astype(
                jnp.bfloat16
            )
            return tile_rows - jnp.dot(scaled, upper_panel, preferred_element_type=jnp.float32)

        pieces = []
        for start in range(0, rows_here, part):
            row_id = (row_start + start) // block
            pieces.append(
                lax.cond(
                    jnp.any(row_id == listed),
                    update_block,
                    unchanged,
                    current[start : start + part],
                    left_panel[start : start + part],
                )
            )
        updated = jnp.concatenate(pieces, axis=0).astype(jnp.bfloat16)
        bit_value = grid_pos >> height & 1
        half_rows = rows_here // 2
        kept = lax.dynamic_slice_in_dim(updated, bit_value * half_rows, half_rows, 0)
        given = lax.dynamic_slice_in_dim(updated, (1 - bit_value) * half_rows, half_rows, 0)
        received = swapped(given, "grid", height)
        current = kept.astype(jnp.float32) + received.astype(jnp.float32)
        row_shift = row_shift + bit_value * half_rows
    return current.astype(jnp.bfloat16)[None]


def solution(mesh):
    return jax.shard_map(
        shards,
        mesh=mesh,
        in_specs=(P("grid", "row", "col"), P(None, "grid", None, "col"), P(None, "grid", None)),
        out_specs=P("grid", "row", "col"),
        check_vma=False,
    )
```

time: 184 us -> 73.8 us (0.40); the launches traced: 185 us -> 73 us
  waiting for transfers between devices: 130 us -> 0 us
  Pallas kernels: 0 us -> 64.9 us
  between operations: 16.9 us -> 1.4 us
  other arithmetic: 17.3 us -> 2.52 us
  starting transfers between devices: 11.8 us -> 0 us
  local copies, waits for them, and re-layouts: 8.99 us -> 4.23 us
    all_gather x3 -> x0, waiting for transfers between devices: 106 us -> none  [the longest x1 46.1 us: shards(): inverse_full = lax.all_gather(inverse_part, 'col', axis=1, tiled=True)]
    pallas_call x0 -> x1, Pallas kernels: none -> 64.9 us  [first_level(): pl.pallas_call(functools.partial(eliminate_kernel, chunk), out_shape=jax....]
    ppermute x1 -> x0, waiting for transfers between devices: 24 us -> none  [swapped(): return lax.ppermute(block, axis, route)]
    ppermute x1 -> x0, starting transfers between devices: 11.8 us -> none  [swapped(): return lax.ppermute(block, axis, route)]
    convert_element_type x2 -> x0, other arithmetic: 6.18 us -> none  [the longest x1 4.02 us: shards(): current = schur[0].astype(jnp.float32)]
    slice x2 -> x0, local copies, waits for them, and re-layouts: 4.27 us -> none  [the longest x1 3.66 us: shards(): tile_rows = current[position * block:(position + 1) * block]]
    another operation x4 -> x0, other arithmetic: 3.92 us -> none
    broadcast_in_dim x1 -> x0, other arithmetic: 2.59 us -> none  [shards(): return current.astype(jnp.bfloat16)[None]]
  transfers between devices with their start and end apart: 4 -> 0, of which waited for: 4 -> 0; matrix products, arithmetic and copies ran while one was open for 5% -> 0% of each run, Pallas kernels for 0% -> 0%
where the time goes in v1:
time: 73.8 us; the launch traced here: 73 us
  Pallas kernels  64.9 us (88%)
  local copies, waits for them, and re-layouts  4.23 us (6%)
  other arithmetic  2.52 us (3%)
  between operations  1.4 us (2%)
    pallas_call x1, Pallas kernels, first_level(): pl.pallas_call(functools.partial(eliminate_kernel, chunk), out_shape=jax....  64.9 us
    unnamed x5, local copies, waits for them, and re-layouts  2.01 us
    dynamic_slice x1, local copies, waits for them, and re-layouts, first_level(): pivots[lax.axis_index('row')] * block - row_start  1.49 us

profile of v1, /device:TPU:0, one launch (start us, length us, event | category | flops | bytes accessed | tf_op | source)
XLA Modules:
  0.0 73.0 jit_solution(6445636471401424628)
XLA Ops:
  0.0 0.0 copy-start
  0.0 1.5 %constant_dynamic-slice_fusion = (s32[1,1,1]{2,1,0:T(1,128)}, s32[1,1,1]{2,1,0:T(1,128)}) fusion(s32[1,1,4]{2,1,0:T(1,128)} %bitcast.15, s32[]{:T(128)S(6)} %select_n.41, s32[]{:T(128)S(6)} %select_n.37), kind=kLoop, calls=%fused_computation.22 | loop fusion | bytes 24 | tf_op jit(solution)/shard_map/dynamic_slice | solution.py:268
  2.8 0.7 slice_bitcast_fusion
  3.6 0.1 compare_reduce_fusion
  3.7 1.2 %bitcast_select_fusion.upper_ref = bf16[256,1024]{1,0:T(8,128)(2,1)S(1)} fusion(bf16[1,1024,1024]{2,1,0:T(8,128)(2,1)} %param.3, s32[]{:T(128)S(6)} %select_n.42, pred[1024]{0:T(1024)(128)(4,1)S(1)} %get-tuple-element.5), kind=kLoop, calls=%fused_computation | loop fusion | flops 262144 | bytes 1049604 | tf_op jit(solution)/shard_map/jit(_where)/select_n | solution.py:270
  4.9 1.2 %bitcast_select_fusion.1.left_ref = bf16[1024,256]{1,0:T(8,128)(2,1)S(1)} fusion(bf16[1,1024,1024]{2,1,0:T(8,128)(2,1)} %param.3, s32[]{:T(128)S(6)} %select_n.38, pred[1024]{0:T(1024)(128)(4,1)S(1)} %get-tuple-element.6), kind=kLoop, calls=%fused_computation.1 | loop fusion | flops 262144 | bytes 1049604 | tf_op jit(solution)/shard_map/jit(_where)/select_n | solution.py:266
  6.1 0.0 copy-done
  6.1 0.0 copy-start.1
  6.1 1.0 %copy-done.1 = bf16[1,1,1024,256]{3,2,1,0:T(8,128)(2,1)S(1)} copy-done((bf16[1,1,1024,256]{3,2,1,0:T(8,128)(2,1)S(1)}, bf16[1,1,1024,256]{3,2,1,0:T(8,128)(2,1)}, u32[]{:S(2)}) %copy-start.1) | copy-done | bytes 524312
  7.2 64.9 %shard_map.37 = bf16[512,1024]{1,0:T(8,128)(2,1)S(1)} custom-call(bf16[1024,1024]{1,0:T(8,128)(2,1)S(1)} %bitcast.12, bf16[1024,256]{1,0:T(8,128)(2,1)S(1)} %bitcast_select_fusion.1.left_ref, bf16[256,1024]{1,0:T(8,128)(2,1)S(1)} %bitcast_select_fusion.upper_ref, bf16[1024,256]{1,0:T(8,128)(2,1)S(1)} %bitcast.14), custom_call_target="tpu_custom_call" | custom-call | tf_op jit(solution)/shard_map/pallas_call | solution.py:274
  72.1 1.0 %copy.5 = bf16[1,512,1024]{2,1,0:T(8,128)(2,1)} copy(bf16[1,512,1024]{2,1,0:T(8,128)(2,1)S(1)} %bitcast.13) | data formatting | bytes 2097152
  (1 shorter events, 0.0 us)
Async XLA Ops:
  0.0 6.1 %copy-start = (bf16[1,1024,1024]{2,1,0:T(8,128)(2,1)S(1)}, bf16[1,1024,1024]{2,1,0:T(8,128)(2,1)}, u32[]{:S(2)}) copy-start(bf16[1,1024,1024]{2,1,0:T(8,128)(2,1)} %param.3) | copy-start | bytes 6291460
  6.1 1.0 %copy-start.1 = (bf16[1,1,1024,256]{3,2,1,0:T(8,128)(2,1)S(1)}, bf16[1,1,1024,256]{3,2,1,0:T(8,128)(2,1)}, u32[]{:S(2)}) copy-start(bf16[1,1,1024,256]{3,2,1,0:T(8,128)(2,1)} %param.4) | copy-start | bytes 1572868

commit v2 on v1

--- a/solution.py
+++ b/solution.py
@@ -79,8 +79,60 @@
             self.copies[s].wait_send()
 
 
+class Relay:
+    def __init__(self, axis, own, place, sems):
+        self.count = lax.axis_size(axis)
+        self.me = lax.axis_index(axis)
+        self.copies = {}
+        for side, step in enumerate((1, -1)):
+            for d in range(self.count - 1):
+                held = jnp.clip(self.me - step * d, 0, self.count - 1)
+                self.copies[side, d] = pltpu.make_async_remote_copy(
+                    src_ref=own if d == 0 else place(held),
+                    dst_ref=place(held),
+                    send_sem=sems[0].at[side, d],
+                    recv_sem=sems[1].at[side, d],
+                    device_id={axis: jnp.clip(self.me + step, 0, self.count - 1)},
+                    device_id_type=MESH,
+                )
+
+    def sends(self, side, d):
+        if side == 0:
+            return (self.me >= d) & (self.me + 1 < self.count)
+        return (self.me + d < self.count) & (self.me >= 1)
+
+    def receives(self, side, d):
+        if side == 0:
+            return self.me >= d + 1
+        return self.me + d + 1 < self.count
+
+    def start(self):
+        for side in range(2):
+            pl.when(self.sends(side, 0))(self.copies[side, 0].start)
+
+    def hop(self, d):
+        for side in range(2):
+            pl.when(self.receives(side, d))(self.copies[side, d].wait_recv)
+            if d + 1 < self.count - 1:
+                pl.when(self.sends(side, d + 1))(self.copies[side, d + 1].start)
+
+    def forward(self):
+        for d in range(self.count - 2):
+            self.hop(d)
+
+    def finish(self):
+        self.hop(self.count - 2)
+
+    def sent(self):
+        for side in range(2):
+            for d in range(self.count - 1):
+                pl.when(self.sends(side, d))(self.copies[side, d].wait_send)
+
+
 def eliminate_kernel(
-    chunk,
+    block,
+    parts,
+    flags,
     tile_ref,
     left_ref,
     upper_ref,
@@ -91,6 +143,7 @@
     upper,
     inv,
     product,
+    change,
     given,
     received,
     local_sems,
@@ -105,40 +158,60 @@
     grid_pos = lax.axis_index("grid")
     n_rows = lax.axis_size("row")
     n_cols = lax.axis_size("col")
-    rows = tile.shape[0]
-    half = rows // 2
-    per_half = half // chunk
+    row_blocks = tile.shape[0] // block
     width = inv.shape[0]
-    piece = left_ref.shape[1]
+    piece = inv_ref.shape[1]
     slab = width // n_rows
+    chunk = block // parts
+    half = row_blocks // 2
     bit_value = lax.rem(grid_pos, 2)
     partner = flipped(grid_pos, 1)
 
-    locals_ = [
-        pltpu.make_async_copy(
-            inv_ref.at[pl.ds(row_pos * slab, slab), :],
-            inv.at[pl.ds(row_pos * slab, slab), pl.ds(pl.multiple_of(col_pos * piece, piece), piece)],
-            local_sems.at[0],
-        ),
-        pltpu.make_async_copy(upper_ref, upper.at[pl.ds(row_pos * slab, slab), :], local_sems.at[1]),
-        pltpu.make_async_copy(
-            left_ref, left.at[:, pl.ds(pl.multiple_of(col_pos * piece, piece), piece)], local_sems.at[2]
-        ),
-        pltpu.make_async_copy(tile_ref, tile, local_sems.at[3]),
-    ]
-    for copy in locals_:
+    inv_copy = pltpu.make_async_copy(
+        inv_ref.at[pl.ds(row_pos * slab, slab), :],
+        inv.at[pl.ds(row_pos * slab, slab), pl.ds(pl.multiple_of(col_pos * piece, piece), piece)],
+        local_sems.at[0],
+    )
+    tile_copy = pltpu.make_async_copy(tile_ref, tile, local_sems.at[1])
+    upper_copy = pltpu.make_async_copy(
+        upper_ref, upper.at[pl.ds(row_pos * slab, slab), :], local_sems.at[2]
+    )
+    left_copy = pltpu.make_async_copy(
+        left_ref,
+        left.at[:, pl.ds(pl.multiple_of(col_pos * piece, piece), piece)],
+        local_sems.at[3],
+    )
+    for copy in (inv_copy, upper_copy, left_copy, tile_copy):
         copy.start()
 
     barrier = pltpu.get_barrier_semaphore()
-    peers = [{"grid": partner}]
-    for axis, count in (("row", n_rows), ("col", n_cols)):
-        bit = 1
-        while bit < count:
-            peers.append({axis: flipped(lax.axis_index(axis), bit)})
-            bit *= 2
-    for peer in peers:
+    bit = 1
+    while bit < n_rows:
+        peer = {"row": flipped(row_pos, bit)}
         pl.semaphore_signal(barrier, inc=1, device_id=peer, device_id_type=MESH)
-    pl.semaphore_wait(barrier, len(peers))
+        bit *= 2
+    pl.semaphore_signal(barrier, inc=1, device_id={"grid": partner}, device_id_type=MESH)
+    for near, there in ((col_pos - 1, col_pos >= 1), (col_pos + 1, col_pos + 1 < n_cols)):
+
+        @pl.when(there)
+        def _():
+            pl.semaphore_signal(
+                barrier,
+                inc=1,
+                device_id={"col": jnp.clip(near, 0, n_cols - 1)},
+                device_id_type=MESH,
+            )
+
+    fixed = n_rows.bit_length()
+    middle = (col_pos >= 1) & (col_pos + 1 < n_cols)
+
+    @pl.when(middle)
+    def _():
+        pl.semaphore_wait(barrier, fixed + 2)
+
+    @pl.when(jnp.logical_not(middle))
+    def _():
+        pl.semaphore_wait(barrier, fixed + 1)
 
     def inv_place(held):
         return inv.at[
@@ -151,23 +224,7 @@
     def upper_place(held):
         return upper.at[pl.ds(held * slab, slab), :]
 
-    starts = [(1 - bit_value) * half + i * chunk for i in range(per_half)]
-    starts += [bit_value * half + i * chunk for i in range(per_half)]
-
-    def left_gather(i):
-        def place(held):
-            return left.at[
-                pl.ds(starts[i], chunk), pl.ds(pl.multiple_of(held * piece, piece), piece)
-            ]
-
-        return Gather(
-            "col",
-            left_ref.at[pl.ds(starts[i], chunk), :],
-            place,
-            (left_sems.at[0, i], left_sems.at[1, i]),
-        )
-
-    inv_col = Gather(
+    inv_col = Relay(
         "col",
         inv_ref.at[pl.ds(row_pos * slab, slab), :],
         inv_place,
@@ -179,71 +236,144 @@
     upper_all = Gather(
         "row", upper_ref, upper_place, (upper_sems.at[0], upper_sems.at[1])
     )
-    lefts = [left_gather(i) for i in range(2 * per_half)]
+
+    def left_gather(unit):
+        def place(held):
+            return left.at[
+                pl.ds(unit * chunk, chunk), pl.ds(pl.multiple_of(held * piece, piece), piece)
+            ]
+
+        return Relay(
+            "col",
+            left_ref.at[pl.ds(unit * chunk, chunk), :],
+            place,
+            (left_sems.at[0, unit], left_sems.at[1, unit]),
+        )
+
+    lefts = [left_gather(unit) for unit in range((row_blocks - 1) * parts)]
+
+    given_start = (1 - bit_value) * half
 
     inv_col.start()
     upper_all.start()
-    lefts[0].start()
+    units = len(lefts)
+    ahead = 2
+    for unit in range(min(ahead, units)):
+        lefts[unit].start()
+    begun = min(ahead, units)
     inv_col.forward()
-    lefts[1].start()
     inv_col.finish()
-    locals_[0].wait()
+    inv_copy.wait()
     inv_row.start()
+    passed = 0
+
+    def pump(upto):
+        nonlocal passed, begun
+        while passed < min(upto, units):
+            if begun < units:
+                lefts[begun].start()
+                begun += 1
+            lefts[passed].forward()
+            passed += 1
+
+    pump(1)
     upper_all.forward()
-    lefts[0].forward()
-    lefts[2].start()
+    pump(2)
     inv_row.forward()
-    lefts[1].forward()
-    lefts[3].start()
+    pump(3)
     upper_all.finish()
     inv_row.finish()
-    locals_[1].wait()
-
-    @pl.loop(0, width // chunk)
+    upper_copy.wait()
+
+    @pl.loop(0, width // block)
     def _(i):
-        at = pl.ds(pl.multiple_of(i * chunk, chunk), chunk)
+        at = pl.ds(pl.multiple_of(i * block, block), block)
         product[at, :] = jnp.dot(
             inv[at, :], upper[...], preferred_element_type=jnp.float32
         ).astype(jnp.bfloat16)
 
-    locals_[2].wait()
-    locals_[3].wait()
-
-    def eliminated(i):
-        at = pl.ds(pl.multiple_of(starts[i], chunk), chunk)
-        change = jnp.dot(left[at, :], product[...], preferred_element_type=jnp.float32)
-        return (tile[at, :].astype(jnp.float32) - change).astype(jnp.bfloat16)
-
+    def eliminated(place, part):
+        row_block = lax.rem(given_start + place, row_blocks)
+        at = pl.ds(pl.multiple_of(row_block * block + part * chunk, chunk), chunk)
+        total = tile[at, :].astype(jnp.float32)
+        if place < row_blocks - 1:
+            total = total - flags[place : place + 1, :] * change[
+                pl.ds(place * block + part * chunk, chunk), :
+            ]
+        if place > 0:
+            total = total - flags[row_blocks + place : row_blocks + place + 1, :] * change[
+                pl.ds((place - 1) * block + part * chunk, chunk), :
+            ]
+        return total.astype(jnp.bfloat16)
+
+    left_copy.wait()
+    tile_copy.wait()
     swaps = []
-    for i in range(2 * per_half):
-        ahead = i + 2
-        if ahead < 2 * per_half:
-            lefts[ahead].forward()
-        if ahead + 2 < 2 * per_half:
-            lefts[ahead + 2].start()
-        lefts[i].finish()
-        if i < per_half:
-            at = pl.ds(i * chunk, chunk)
-            given[at, :] = eliminated(i)
-            swap = pltpu.make_async_remote_copy(
-                src_ref=given.at[at, :],
-                dst_ref=received.at[at, :],
-                send_sem=swap_sems.at[0, i],
-                recv_sem=swap_sems.at[1, i],
-                device_id={"grid": partner},
-                device_id_type=MESH,
-            )
-            swap.start()
-            swaps.append(swap)
-        else:
-            at = pl.ds((i - per_half) * chunk, chunk)
-            kept = eliminated(i).astype(jnp.float32)
-            swaps[i - per_half].wait_recv()
-            out_ref[at, :] = (kept + received[at, :].astype(jnp.float32)).astype(out_ref.dtype)
+    for place in range(row_blocks):
+        for part in range(parts):
+            if place < row_blocks - 1:
+                unit = place * parts + part
+                pump(unit + 1 + 1)
+                lefts[unit].finish()
+                at = pl.ds(unit * chunk, chunk)
+                change[at, :] = jnp.dot(
+                    left[at, :], product[...], preferred_element_type=jnp.float32
+                )
+            if place < half:
+                at = pl.ds(place * block + part * chunk, chunk)
+                given[at, :] = eliminated(place, part)
+                swap = pltpu.make_async_remote_copy(
+                    src_ref=given.at[at, :],
+                    dst_ref=received.at[at, :],
+                    send_sem=swap_sems.at[0, len(swaps)],
+                    recv_sem=swap_sems.at[1, len(swaps)],
+                    device_id={"grid": partner},
+                    device_id_type=MESH,
+                )
+                swap.start()
+                swaps.append(swap)
+            else:
+                at = pl.ds((place - half) * block + part * chunk, chunk)
+                kept = eliminated(place, part).astype(jnp.float32)
+                swaps[(place - half) * parts + part].wait_recv()
+                out_ref[at, :] = (kept + received[at, :].astype(jnp.float32)).astype(out_ref.dtype)
     for gather in [inv_col, inv_row, upper_all] + lefts:
         gather.sent()
     for swap in swaps:
         swap.wait_send()
+
+
+def cut_kernel(block, chosen, left_ref, upper_ref, left_out, upper_out, flags_out):
+    row_pos = lax.axis_index("row")
+    col_pos = lax.axis_index("col")
+    n_rows = lax.axis_size("row")
+    row_blocks = left_ref.shape[0] // block
+    col_blocks = upper_ref.shape[1] // block
+
+    def is_listed(number):
+        found = jnp.int32(0)
+        for k in range(n_rows, chosen.shape[0]):
+            found = found + (chosen[k] == number).astype(jnp.int32)
+        return found.astype(jnp.float32)
+
+    given_start = (1 - lax.rem(lax.axis_index("grid"), 2)) * (row_blocks // 2)
+    own_row = lax.rem(chosen[row_pos], row_blocks)
+    pivot_place = lax.rem(own_row + row_blocks - given_start, row_blocks)
+    for slot in range(row_blocks - 1):
+        place = slot + (slot >= pivot_place).astype(jnp.int32)
+        row_block = lax.rem(given_start + place, row_blocks)
+        values = left_ref[pl.ds(pl.multiple_of(row_block * block, block), block), :]
+        kept = values.astype(jnp.float32) * is_listed(row_pos * row_blocks + row_block)
+        left_out[pl.ds(slot * block, block), :] = kept.astype(left_out.dtype)
+    for c in range(col_blocks):
+        span = pl.ds(c * block, block)
+        kept = upper_ref[:, span].astype(jnp.float32) * is_listed(col_pos * col_blocks + c)
+        upper_out[:, span] = kept.astype(upper_out.dtype)
+    for place in range(row_blocks):
+        for row, holds in ((place, pivot_place > place), (row_blocks + place, pivot_place < place)):
+            flags_out[row : row + 1, :] = jnp.full(
+                (1, flags_out.shape[1]), holds.astype(jnp.int32).astype(jnp.float32)
+            )
 
 
 def first_level(tile, inverse, chosen, out_dtype):
@@ -252,49 +382,62 @@
     rows, cols = tile.shape
     width = inverse.shape[0]
     block = width // n_rows
-    row_start = lax.axis_index("row") * rows
-    col_pos = lax.axis_index("col")
-    col_start = col_pos * cols
-    pivots = chosen[:n_rows]
-    listed = chosen[n_rows:]
-    row_ids = (row_start + jnp.arange(rows, dtype=jnp.int32)) // block
-    col_ids = (col_start + jnp.arange(cols, dtype=jnp.int32)) // block
-    row_keep = jnp.any(row_ids[:, None] == listed[None, :], axis=1)
-    col_keep = jnp.any(col_ids[:, None] == listed[None, :], axis=1)
-    zero = jnp.zeros((), tile.dtype)
-    left = lax.dynamic_slice_in_dim(tile, pivots[col_pos] * block - col_start, block, 1)
-    left = jnp.where(row_keep[:, None], left, zero)
-    upper = lax.dynamic_slice_in_dim(
-        tile, pivots[lax.axis_index("row")] * block - row_start, block, 0
-    )
-    upper = jnp.where(col_keep[None, :], upper, zero)
-    chunk = rows // 4
+    slots = rows // block - 1
+    parts = 2
     bf16 = jnp.bfloat16
     dma = pltpu.SemaphoreType.DMA
+    left, upper, flags = pl.pallas_call(
+        functools.partial(cut_kernel, block),
+        grid_spec=pltpu.PrefetchScalarGridSpec(
+            num_scalar_prefetch=1,
+            grid=(1,),
+            in_specs=[
+                pl.BlockSpec(
+                    (rows, block),
+                    lambda i, chosen: (0, lax.rem(chosen[lax.axis_index("col")], cols // block)),
+                ),
+                pl.BlockSpec(
+                    (block, cols),
+                    lambda i, chosen: (lax.rem(chosen[lax.axis_index("row")], rows // block), 0),
+                ),
+            ],
+            out_specs=[
+                pl.BlockSpec((slots * block, block), lambda i, chosen: (0, 0)),
+                pl.BlockSpec((block, cols), lambda i, chosen: (0, 0)),
+                pl.BlockSpec((2 * (slots + 1), cols), lambda i, chosen: (0, 0)),
+            ],
+        ),
+        out_shape=[
+            jax.ShapeDtypeStruct((slots * block, block), bf16),
+            jax.ShapeDtypeStruct((block, cols), bf16),
+            jax.ShapeDtypeStruct((2 * (slots + 1), cols), jnp.float32),
+        ],
+    )(chosen, tile, tile)
     return pl.pallas_call(
-        functools.partial(eliminate_kernel, chunk),
+        functools.partial(eliminate_kernel, block, parts),
         out_shape=jax.ShapeDtypeStruct((rows // 2, cols), out_dtype),
-        in_specs=[pl.BlockSpec(memory_space=pl.ANY)] * 4,
+        in_specs=[pl.BlockSpec(memory_space=pltpu.VMEM)] + [pl.BlockSpec(memory_space=pl.ANY)] * 4,
         out_specs=pl.BlockSpec(memory_space=pltpu.VMEM),
         scratch_shapes=[
             pltpu.VMEM((rows, cols), bf16),
-            pltpu.VMEM((rows, width), bf16),
+            pltpu.VMEM((slots * block, width), bf16),
             pltpu.VMEM((width, cols), bf16),
             pltpu.VMEM((width, width), bf16),
             pltpu.VMEM((width, cols), bf16),
+            pltpu.VMEM((slots * block, cols), jnp.float32),
             pltpu.VMEM((rows // 2, cols), bf16),
             pltpu.VMEM((rows // 2, cols), bf16),
             dma((4,)),
-            dma((2, n_cols - 1)),
+            dma((2, 2, n_cols - 1)),
             dma((2, n_rows - 1)),
             dma((2, n_rows - 1)),
-            dma((2, 4, n_cols - 1)),
-            dma((2, 2)),
+            dma((2, slots * parts, 2, n_cols - 1)),
+            dma((2, (slots + 1) // 2 * parts)),
         ],
         compiler_params=pltpu.CompilerParams(
-            collective_id=0, has_side_effects=True, vmem_limit_bytes=40 * 1024 * 1024
+            collective_id=0, has_side_effects=True, vmem_limit_bytes=56 * 1024 * 1024
         ),
-    )(tile, left, upper, inverse)
+    )(flags, tile, left, upper, inverse)
 
 
 def shards(schur, d_inv, blocks):

time: 73.8 us -> 68.2 us (0.924)
  other arithmetic: 2.52 us -> 0 us
  local copies, waits for them, and re-layouts: 4.23 us -> 2.26 us
  between operations: 1.4 us -> 0.01 us
  Pallas kernels: 64.9 us -> 65.7 us
    select_n x3 -> x0, other arithmetic: 2.42 us -> none  [the longest x1 1.25 us: first_level(): left = jnp.where(row_keep[:, None], left, zero)]
    dynamic_slice x1 -> x0, local copies, waits for them, and re-layouts: 1.49 us -> none  [first_level(): pivots[lax.axis_index('row')] * block - row_start]
    pallas_call x1 -> x2, Pallas kernels: 64.9 us -> 65.7 us  [the longest x1 62.7 us: first_level(): pl.pallas_call(functools.partial(eliminate_kernel, block, parts), out_sha...]
    unnamed x5 -> x1, local copies, waits for them, and re-layouts: 2.01 us -> 2.26 us
where the time goes in v2:
time: 68.2 us; the launch traced here: 67.9 us
  Pallas kernels  65.7 us (96%)
  local copies, waits for them, and re-layouts  2.26 us (3%)
    pallas_call x1, Pallas kernels, first_level(): pl.pallas_call(functools.partial(eliminate_kernel, block, parts), out_sha...  62.7 us
    pallas_call x1, Pallas kernels, first_level(): pl.pallas_call(functools.partial(cut_kernel, block), grid_spec=pltpu.Pref...  2.93 us
    unnamed x1, local copies, waits for them, and re-layouts  2.26 us

profile of v2, /device:TPU:0, one launch (start us, length us, event | category | flops | bytes accessed | tf_op | source)
XLA Modules:
  0.0 67.9 jit_solution(13987493592355351436)
XLA Ops:
  0.0 2.9 %shard_map.37 = (bf16[768,256]{1,0:T(8,128)(2,1)}, bf16[256,1024]{1,0:T(8,128)(2,1)}, f32[8,1024]{1,0:T(8,128)}) custom-call(s32[12]{0:T(128)} %bitcast.9, bf16[1024,1024]{1,0:T(8,128)(2,1)} %bitcast.4, bf16[1024,1024]{1,0:T(8,128)(2,1)} %bitcast.5), custom_call_target="tpu_custom_call" | custom-call | tf_op jit(solution)/shard_map/pallas_call | solution.py:389
  2.9 62.7 %shard_map.38 = bf16[512,1024]{1,0:T(8,128)(2,1)} custom-call(f32[8,1024]{1,0:T(8,128)} %get-tuple-element.8.flags, bf16[1024,1024]{1,0:T(8,128)(2,1)} %bitcast.6, bf16[768,256]{1,0:T(8,128)(2,1)} %get-tuple-element.9.left_ref, bf16[256,1024]{1,0:T(8,128)(2,1)} %get-tuple-element.10.upper_ref, bf16[1024,256]{1,0:T(8,128)(2,1)} %bitcast.8), custom_call_target="tpu_custom_call" | custom-call | tf_op jit(solution)/shard_map/pallas_call | solution.py:416
  65.7 2.3 %copy.5 = bf16[1,512,1024]{2,1,0:T(8,128)(2,1)} copy(bf16[1,512,1024]{2,1,0:T(8,128)(2,1)} %bitcast.7) | data formatting | bytes 2097152

commit v3 on v2

--- a/solution.py
+++ b/solution.py
@@ -136,6 +136,7 @@
     tile_ref,
     left_ref,
     upper_ref,
+    raw_ref,
     inv_ref,
     out_ref,
     tile,
@@ -146,12 +147,15 @@
     change,
     given,
     received,
+    raw,
+    other_flags,
     local_sems,
     inv_col_sems,
-    inv_row_sems,
+    product_all_sems,
     upper_sems,
     left_sems,
     swap_sems,
+    early_sems,
 ):
     row_pos = lax.axis_index("row")
     col_pos = lax.axis_index("col")
@@ -159,7 +163,8 @@
     n_rows = lax.axis_size("row")
     n_cols = lax.axis_size("col")
     row_blocks = tile.shape[0] // block
-    width = inv.shape[0]
+    col_blocks = tile.shape[1] // block
+    width = inv.shape[1]
     piece = inv_ref.shape[1]
     slab = width // n_rows
     chunk = block // parts
@@ -169,7 +174,7 @@
 
     inv_copy = pltpu.make_async_copy(
         inv_ref.at[pl.ds(row_pos * slab, slab), :],
-        inv.at[pl.ds(row_pos * slab, slab), pl.ds(pl.multiple_of(col_pos * piece, piece), piece)],
+        inv.at[:, pl.ds(pl.multiple_of(col_pos * piece, piece), piece)],
         local_sems.at[0],
     )
     tile_copy = pltpu.make_async_copy(tile_ref, tile, local_sems.at[1])
@@ -214,12 +219,10 @@
         pl.semaphore_wait(barrier, fixed + 1)
 
     def inv_place(held):
-        return inv.at[
-            pl.ds(row_pos * slab, slab), pl.ds(pl.multiple_of(held * piece, piece), piece)
-        ]
+        return inv.at[:, pl.ds(pl.multiple_of(held * piece, piece), piece)]
 
     def slab_place(held):
-        return inv.at[pl.ds(held * slab, slab), :]
+        return product.at[pl.ds(held * slab, slab), :]
 
     def upper_place(held):
         return upper.at[pl.ds(held * slab, slab), :]
@@ -230,8 +233,8 @@
         inv_place,
         (inv_col_sems.at[0], inv_col_sems.at[1]),
     )
-    inv_row = Gather(
-        "row", slab_place(row_pos), slab_place, (inv_row_sems.at[0], inv_row_sems.at[1])
+    product_all = Gather(
+        "row", slab_place(row_pos), slab_place, (product_all_sems.at[0], product_all_sems.at[1])
     )
     upper_all = Gather(
         "row", upper_ref, upper_place, (upper_sems.at[0], upper_sems.at[1])
@@ -256,15 +259,27 @@
 
     inv_col.start()
     upper_all.start()
+    early = [
+        pltpu.make_async_remote_copy(
+            src_ref=source,
+            dst_ref=target,
+            send_sem=early_sems.at[0, i],
+            recv_sem=early_sems.at[1, i],
+            device_id={"grid": partner},
+            device_id_type=MESH,
+        )
+        for i, (source, target) in enumerate(
+            ((raw_ref, raw), (flags.at[pl.ds(16, 16), :], other_flags))
+        )
+    ]
+    for copy in early:
+        copy.start()
     units = len(lefts)
     ahead = 2
     for unit in range(min(ahead, units)):
         lefts[unit].start()
     begun = min(ahead, units)
     inv_col.forward()
-    inv_col.finish()
-    inv_copy.wait()
-    inv_row.start()
     passed = 0
 
     def pump(upto):
@@ -276,35 +291,53 @@
             lefts[passed].forward()
             passed += 1
 
+    upper_all.forward()
+    inv_col.finish()
+    inv_copy.wait()
     pump(1)
-    upper_all.forward()
+    upper_all.finish()
+    upper_copy.wait()
+    product[pl.ds(row_pos * slab, slab), :] = jnp.dot(
+        inv[...], upper[...], preferred_element_type=jnp.float32
+    ).astype(jnp.bfloat16)
+    product_all.start()
     pump(2)
-    inv_row.forward()
+    product_all.forward()
     pump(3)
-    upper_all.finish()
-    inv_row.finish()
-    upper_copy.wait()
-
-    @pl.loop(0, width // block)
-    def _(i):
-        at = pl.ds(pl.multiple_of(i * block, block), block)
-        product[at, :] = jnp.dot(
-            inv[at, :], upper[...], preferred_element_type=jnp.float32
-        ).astype(jnp.bfloat16)
-
-    def eliminated(place, part):
+    product_all.finish()
+
+    def pick(flag_ref, start, q):
+        return flag_ref[start + q : start + q + 1, :]
+
+    def columns(ref, at, q):
+        return ref[at, q * block : (q + 1) * block].astype(jnp.float32)
+
+    def tile_rows(place, part):
         row_block = lax.rem(given_start + place, row_blocks)
-        at = pl.ds(pl.multiple_of(row_block * block + part * chunk, chunk), chunk)
-        total = tile[at, :].astype(jnp.float32)
+        return pl.ds(pl.multiple_of(row_block * block + part * chunk, chunk), chunk)
+
+    def change_at(place, part, slot):
+        total = None
         if place < row_blocks - 1:
-            total = total - flags[place : place + 1, :] * change[
-                pl.ds(place * block + part * chunk, chunk), :
-            ]
+            at = pl.ds(place * block + part * chunk, chunk)
+            total = pick(flags, 0, place) * columns(change, at, slot)
         if place > 0:
-            total = total - flags[row_blocks + place : row_blocks + place + 1, :] * change[
-                pl.ds((place - 1) * block + part * chunk, chunk), :
-            ]
-        return total.astype(jnp.bfloat16)
+            at = pl.ds((place - 1) * block + part * chunk, chunk)
+            term = pick(flags, row_blocks, place) * columns(change, at, slot)
+            total = term if total is None else total + term
+        return total
+
+    def spread(flag_ref, start, slots):
+        placed = []
+        for q in range(col_blocks):
+            total = None
+            if q < col_blocks - 1:
+                total = pick(flag_ref, start, q) * slots[q]
+            if q > 0:
+                term = pick(flag_ref, start + col_blocks, q) * slots[q - 1]
+                total = term if total is None else total + term
+            placed.append(total)
+        return placed
 
     left_copy.wait()
     tile_copy.wait()
@@ -321,7 +354,13 @@
                 )
             if place < half:
                 at = pl.ds(place * block + part * chunk, chunk)
-                given[at, :] = eliminated(place, part)
+                rows_at = tile_rows(place, part)
+                for slot in range(col_blocks - 1):
+                    first = pick(flags, 16, slot)
+                    kept = first * columns(tile, rows_at, slot)
+                    kept = kept + (1.0 - first) * columns(tile, rows_at, slot + 1)
+                    kept = kept - change_at(place, part, slot)
+                    given[at, slot * block : (slot + 1) * block] = kept.astype(given.dtype)
                 swap = pltpu.make_async_remote_copy(
                     src_ref=given.at[at, :],
                     dst_ref=received.at[at, :],
@@ -334,16 +373,32 @@
                 swaps.append(swap)
             else:
                 at = pl.ds((place - half) * block + part * chunk, chunk)
-                kept = eliminated(place, part).astype(jnp.float32)
+                rows_at = tile_rows(place, part)
+                own = spread(
+                    flags, 16, [change_at(place, part, c) for c in range(col_blocks - 1)]
+                )
+                if place == half and part == 0:
+                    for copy in early:
+                        copy.wait_recv()
                 swaps[(place - half) * parts + part].wait_recv()
-                out_ref[at, :] = (kept + received[at, :].astype(jnp.float32)).astype(out_ref.dtype)
-    for gather in [inv_col, inv_row, upper_all] + lefts:
+                other = spread(
+                    other_flags, 0, [columns(received, at, c) for c in range(col_blocks - 1)]
+                )
+                for q in range(col_blocks):
+                    kept = (columns(tile, rows_at, q) - own[q]).astype(jnp.bfloat16)
+                    term = other[q] + pick(other_flags, 2 * col_blocks, q) * columns(raw, at, 0)
+                    out_ref[at, q * block : (q + 1) * block] = (
+                        kept.astype(jnp.float32) + term
+                    ).astype(out_ref.dtype)
+    for copy in early:
+        copy.wait_send()
+    for gather in [inv_col, product_all, upper_all] + lefts:
         gather.sent()
     for swap in swaps:
         swap.wait_send()
 
 
-def cut_kernel(block, chosen, left_ref, upper_ref, left_out, upper_out, flags_out):
+def cut_kernel(block, chosen, left_ref, upper_ref, left_out, upper_out, raw_out, flags_out):
     row_pos = lax.axis_index("row")
     col_pos = lax.axis_index("col")
     n_rows = lax.axis_size("row")
@@ -365,15 +420,27 @@
         values = left_ref[pl.ds(pl.multiple_of(row_block * block, block), block), :]
         kept = values.astype(jnp.float32) * is_listed(row_pos * row_blocks + row_block)
         left_out[pl.ds(slot * block, block), :] = kept.astype(left_out.dtype)
-    for c in range(col_blocks):
-        span = pl.ds(c * block, block)
-        kept = upper_ref[:, span].astype(jnp.float32) * is_listed(col_pos * col_blocks + c)
-        upper_out[:, span] = kept.astype(upper_out.dtype)
+    raw_rows = row_blocks // 2 * block
+    raw_out[...] = left_ref[pl.ds(pl.multiple_of(given_start * block, block), raw_rows), :]
+    own_col = lax.rem(chosen[col_pos], col_blocks)
+    for slot in range(col_blocks - 1):
+        c = slot + (slot >= own_col).astype(jnp.int32)
+        values = upper_ref[:, pl.ds(pl.multiple_of(c * block, block), block)]
+        kept = values.astype(jnp.float32) * is_listed(col_pos * col_blocks + c)
+        upper_out[:, slot * block : (slot + 1) * block] = kept.astype(upper_out.dtype)
+    flags_out[...] = jnp.zeros_like(flags_out)
+    rows_of = []
     for place in range(row_blocks):
-        for row, holds in ((place, pivot_place > place), (row_blocks + place, pivot_place < place)):
-            flags_out[row : row + 1, :] = jnp.full(
-                (1, flags_out.shape[1]), holds.astype(jnp.int32).astype(jnp.float32)
-            )
+        rows_of.append((place, pivot_place > place))
+        rows_of.append((row_blocks + place, pivot_place < place))
+    for q in range(col_blocks):
+        rows_of.append((16 + q, own_col > q))
+        rows_of.append((16 + col_blocks + q, own_col < q))
+        rows_of.append((16 + 2 * col_blocks + q, own_col == q))
+    for row, holds in rows_of:
+        flags_out[row : row + 1, :] = jnp.full(
+            (1, flags_out.shape[1]), holds.astype(jnp.int32).astype(jnp.float32)
+        )
 
 
 def first_level(tile, inverse, chosen, out_dtype):
@@ -383,10 +450,11 @@
     width = inverse.shape[0]
     block = width // n_rows
     slots = rows // block - 1
+    narrow = cols - block
     parts = 2
     bf16 = jnp.bfloat16
     dma = pltpu.SemaphoreType.DMA
-    left, upper, flags = pl.pallas_call(
+    left, upper, raw, flags = pl.pallas_call(
         functools.partial(cut_kernel, block),
         grid_spec=pltpu.PrefetchScalarGridSpec(
             num_scalar_prefetch=1,
@@ -403,41 +471,46 @@
             ],
             out_specs=[
                 pl.BlockSpec((slots * block, block), lambda i, chosen: (0, 0)),
-                pl.BlockSpec((block, cols), lambda i, chosen: (0, 0)),
-                pl.BlockSpec((2 * (slots + 1), cols), lambda i, chosen: (0, 0)),
+                pl.BlockSpec((block, narrow), lambda i, chosen: (0, 0)),
+                pl.BlockSpec((rows // 2, block), lambda i, chosen: (0, 0)),
+                pl.BlockSpec((32, block), lambda i, chosen: (0, 0)),
             ],
         ),
         out_shape=[
             jax.ShapeDtypeStruct((slots * block, block), bf16),
-            jax.ShapeDtypeStruct((block, cols), bf16),
-            jax.ShapeDtypeStruct((2 * (slots + 1), cols), jnp.float32),
+            jax.ShapeDtypeStruct((block, narrow), bf16),
+            jax.ShapeDtypeStruct((rows // 2, block), bf16),
+            jax.ShapeDtypeStruct((32, block), jnp.float32),
         ],
     )(chosen, tile, tile)
     return pl.pallas_call(
         functools.partial(eliminate_kernel, block, parts),
         out_shape=jax.ShapeDtypeStruct((rows // 2, cols), out_dtype),
-        in_specs=[pl.BlockSpec(memory_space=pltpu.VMEM)] + [pl.BlockSpec(memory_space=pl.ANY)] * 4,
+        in_specs=[pl.BlockSpec(memory_space=pltpu.VMEM)] + [pl.BlockSpec(memory_space=pl.ANY)] * 5,
         out_specs=pl.BlockSpec(memory_space=pltpu.VMEM),
         scratch_shapes=[
             pltpu.VMEM((rows, cols), bf16),
             pltpu.VMEM((slots * block, width), bf16),
-            pltpu.VMEM((width, cols), bf16),
-            pltpu.VMEM((width, width), bf16),
-            pltpu.VMEM((width, cols), bf16),
-            pltpu.VMEM((slots * block, cols), jnp.float32),
-            pltpu.VMEM((rows // 2, cols), bf16),
-            pltpu.VMEM((rows // 2, cols), bf16),
+            pltpu.VMEM((width, narrow), bf16),
+            pltpu.VMEM((block, width), bf16),
+            pltpu.VMEM((width, narrow), bf16),
+            pltpu.VMEM((slots * block, narrow), jnp.float32),
+            pltpu.VMEM((rows // 2, narrow), bf16),
+            pltpu.VMEM((rows // 2, narrow), bf16),
+            pltpu.VMEM((rows // 2, block), bf16),
+            pltpu.VMEM((16, block), jnp.float32),
             dma((4,)),
             dma((2, 2, n_cols - 1)),
             dma((2, n_rows - 1)),
             dma((2, n_rows - 1)),
             dma((2, slots * parts, 2, n_cols - 1)),
             dma((2, (slots + 1) // 2 * parts)),
+            dma((2, 2)),
         ],
         compiler_params=pltpu.CompilerParams(
             collective_id=0, has_side_effects=True, vmem_limit_bytes=56 * 1024 * 1024
         ),
-    )(flags, tile, left, upper, inverse)
+    )(flags, tile, left, upper, raw, inverse)
 
 
 def shards(schur, d_inv, blocks):

time: 68.2 us -> 60.3 us (0.88)
  Pallas kernels: 65.7 us -> 57.8 us
    pallas_call x1, Pallas kernels: 62.7 us -> 54.9 us  [first_level(): pl.pallas_call(functools.partial(eliminate_kernel, block, parts), out_sha...]
where the time goes in v3:
time: 60.3 us; the launch traced here: 60.1 us
  Pallas kernels  57.8 us (96%)
  local copies, waits for them, and re-layouts  2.26 us (4%)
    pallas_call x1, Pallas kernels, first_level(): pl.pallas_call(functools.partial(eliminate_kernel, block, parts), out_sha...  54.9 us
    pallas_call x1, Pallas kernels, first_level(): pl.pallas_call(functools.partial(cut_kernel, block), grid_spec=pltpu.Pref...  2.94 us
    unnamed x1, local copies, waits for them, and re-layouts  2.26 us

profile of v3, /device:TPU:0, one launch (start us, length us, event | category | flops | bytes accessed | tf_op | source)
XLA Modules:
  0.0 60.1 jit_solution(8438064575396170866)
XLA Ops:
  0.0 2.9 %shard_map.37 = (bf16[768,256]{1,0:T(8,128)(2,1)}, bf16[256,768]{1,0:T(8,128)(2,1)}, bf16[512,256]{1,0:T(8,128)(2,1)}, f32[32,256]{1,0:T(8,128)}) custom-call(s32[12]{0:T(128)} %bitcast.9, bf16[1024,1024]{1,0:T(8,128)(2,1)} %bitcast.4, bf16[1024,1024]{1,0:T(8,128)(2,1)} %bitcast.5), custom_call_target="tpu_custom_call" | custom-call | tf_op jit(solution)/shard_map/pallas_call | solution.py:457
  2.9 54.9 %shard_map.38 = bf16[512,1024]{1,0:T(8,128)(2,1)} custom-call(f32[32,256]{1,0:T(8,128)} %get-tuple-element.9.flags, bf16[1024,1024]{1,0:T(8,128)(2,1)} %bitcast.6, bf16[768,256]{1,0:T(8,128)(2,1)} %get-tuple-element.10.left_ref, bf16[256,768]{1,0:T(8,128)(2,1)} %get-tuple-element.11.upper_ref, bf16[512,256]{1,0:T(8,128)(2,1)} %get-tuple-element.12.raw_ref, ...), custom_call_target="tpu_custom_call" | custom-call | tf_op jit(solution)/shard_map/pallas_call | solution.py:486
  57.8 2.3 %copy.5 = bf16[1,512,1024]{2,1,0:T(8,128)(2,1)} copy(bf16[1,512,1024]{2,1,0:T(8,128)(2,1)} %bitcast.7) | data formatting | bytes 2097152

commit v4 on v3

--- a/solution.py
+++ b/solution.py
@@ -196,27 +196,10 @@
         pl.semaphore_signal(barrier, inc=1, device_id=peer, device_id_type=MESH)
         bit *= 2
     pl.semaphore_signal(barrier, inc=1, device_id={"grid": partner}, device_id_type=MESH)
-    for near, there in ((col_pos - 1, col_pos >= 1), (col_pos + 1, col_pos + 1 < n_cols)):
-
-        @pl.when(there)
-        def _():
-            pl.semaphore_signal(
-                barrier,
-                inc=1,
-                device_id={"col": jnp.clip(near, 0, n_cols - 1)},
-                device_id_type=MESH,
-            )
-
-    fixed = n_rows.bit_length()
-    middle = (col_pos >= 1) & (col_pos + 1 < n_cols)
-
-    @pl.when(middle)
-    def _():
-        pl.semaphore_wait(barrier, fixed + 2)
-
-    @pl.when(jnp.logical_not(middle))
-    def _():
-        pl.semaphore_wait(barrier, fixed + 1)
+    for apart in range(1, n_cols):
+        peer = {"col": lax.rem(col_pos + apart, n_cols)}
+        pl.semaphore_signal(barrier, inc=1, device_id=peer, device_id_type=MESH)
+    pl.semaphore_wait(barrier, n_rows.bit_length() + n_cols - 1)
 
     def inv_place(held):
         return inv.at[:, pl.ds(pl.multiple_of(held * piece, piece), piece)]
@@ -227,11 +210,11 @@
     def upper_place(held):
         return upper.at[pl.ds(held * slab, slab), :]
 
-    inv_col = Relay(
+    inv_col = Gather(
         "col",
         inv_ref.at[pl.ds(row_pos * slab, slab), :],
         inv_place,
-        (inv_col_sems.at[0], inv_col_sems.at[1]),
+        (inv_col_sems.at[0, 0], inv_col_sems.at[1, 0]),
     )
     product_all = Gather(
         "row", slab_place(row_pos), slab_place, (product_all_sems.at[0], product_all_sems.at[1])
@@ -294,7 +277,6 @@
     upper_all.forward()
     inv_col.finish()
     inv_copy.wait()
-    pump(1)
     upper_all.finish()
     upper_copy.wait()
     product[pl.ds(row_pos * slab, slab), :] = jnp.dot(

time: 60.3 us -> 58.5 us (0.970)
  Pallas kernels: 57.8 us -> 56 us
    pallas_call x1, Pallas kernels: 54.9 us -> 53.1 us  [first_level(): pl.pallas_call(functools.partial(eliminate_kernel, block, parts), out_sha...]
where the time goes in v4:
time: 58.5 us; the launch traced here: 58.3 us
  Pallas kernels  56 us (96%)
  local copies, waits for them, and re-layouts  2.26 us (4%)
    pallas_call x1, Pallas kernels, first_level(): pl.pallas_call(functools.partial(eliminate_kernel, block, parts), out_sha...  53.1 us
    pallas_call x1, Pallas kernels, first_level(): pl.pallas_call(functools.partial(cut_kernel, block), grid_spec=pltpu.Pref...  2.94 us
    unnamed x1, local copies, waits for them, and re-layouts  2.26 us

profile of v4, /device:TPU:0, one launch (start us, length us, event | category | flops | bytes accessed | tf_op | source)
XLA Modules:
  0.0 58.3 jit_solution(15609594546991850247)
XLA Ops:
  0.0 2.9 %shard_map.37 = (bf16[768,256]{1,0:T(8,128)(2,1)}, bf16[256,768]{1,0:T(8,128)(2,1)}, bf16[512,256]{1,0:T(8,128)(2,1)}, f32[32,256]{1,0:T(8,128)}) custom-call(s32[12]{0:T(128)} %bitcast.9, bf16[1024,1024]{1,0:T(8,128)(2,1)} %bitcast.4, bf16[1024,1024]{1,0:T(8,128)(2,1)} %bitcast.5), custom_call_target="tpu_custom_call" | custom-call | tf_op jit(solution)/shard_map/pallas_call | solution.py:439
  2.9 53.1 %shard_map.38 = bf16[512,1024]{1,0:T(8,128)(2,1)} custom-call(f32[32,256]{1,0:T(8,128)} %get-tuple-element.9.flags, bf16[1024,1024]{1,0:T(8,128)(2,1)} %bitcast.6, bf16[768,256]{1,0:T(8,128)(2,1)} %get-tuple-element.10.left_ref, bf16[256,768]{1,0:T(8,128)(2,1)} %get-tuple-element.11.upper_ref, bf16[512,256]{1,0:T(8,128)(2,1)} %get-tuple-element.12.raw_ref, ...), custom_call_target="tpu_custom_call" | custom-call | tf_op jit(solution)/shard_map/pallas_call | solution.py:468
  56.0 2.3 %copy.5 = bf16[1,512,1024]{2,1,0:T(8,128)(2,1)} copy(bf16[1,512,1024]{2,1,0:T(8,128)(2,1)} %bitcast.7) | data formatting | bytes 2097152
